TPU v7x, 32 devices: a whole 2x2x4 slice. The times are simulated.
32 devices in a mesh: row: 4 (over z), col: 8 (over y, x, core).
Axes of the slice: x: 2, y: 2, z: 4, core: 2. Of those that a mesh axis runs over, the one named last changes fastest.
Arguments:
- a_matrix: float32 [1024, 3072], P('row', 'col'), may hold values from -6 to 6
- b_matrix: float32 [1024, 3072], P('row', 'col'), as said below
Outputs:
- a_result: float32 [1024, 3072], P('row', 'col')
- b_result: float32 [1024, 3072], P('row', 'col')
Inputs may be any that keep to these rules, and one draw needn't show every extreme that they name: b_matrix is zero in its first 256 columns and, at the window's columns t, zero in rows below t; its entry in row t at window column t lies between 4 and 8.
All inputs are finite; a program needn't handle non-finite values.
Results may differ from a plain program's by a relative error of at most 0.00023.
Values sent between devices are 32-bit elements; how exact they have to be, the bound alone decides.
A program may use at most 64 MiB of HBM per device.

v0:
```python
import functools

import jax
import jax.numpy as jnp
from jax import lax
from jax.experimental import pallas as pl
from jax.experimental.pallas import tpu as pltpu
from jax.sharding import PartitionSpec as P

NB = 256
HB = NB // 2
TILE = 8
COUNT = HB // TILE
MESH = pl.DeviceIdType.MESH
VM = pl.BlockSpec(memory_space=pltpu.VMEM)
LIMIT = 32 * 1024 * 1024


def dot(x, y, cx=1, cy=0):
    return lax.dot_general(
        x,
        y,
        (((cx,), (cy,)), ((), ())),
        precision=lax.Precision.HIGHEST,
        preferred_element_type=jnp.float32,
    )


def spread(x):
    return jnp.broadcast_to(x, (TILE, HB))


def stack(rows):
    sub = lax.broadcasted_iota(jnp.int32, (TILE, HB), 0)
    out = rows[0]
    for k in range(1, TILE):
        out = jnp.where(sub == k, rows[k], out)
    return out


def apply_tile(tile, t, rows, inside):
    out = jnp.where(inside, 0.0, tile)
    for k in range(TILE):
        out = out - spread(tile[:, t * TILE + k : t * TILE + k + 1]) * rows[k]
    return out


def step(tiles, t, order, symmetric, room):
    lane = lax.broadcasted_iota(jnp.int32, (TILE, HB), 1) - t * TILE
    inside = (lane >= 0) & (lane < TILE)
    at = [lane == k for k in range(TILE)]
    place = {m: i for i, m in enumerate(order)}
    used = lambda r, k: not symmetric or place[r] <= place[k]
    rows = [spread(tiles[t][k : k + 1, :]) for k in range(TILE)]
    for k in range(TILE):
        room[k * TILE : (k + 1) * TILE, :] = spread(tiles[t][:, t * TILE + k : t * TILE + k + 1])
    s = [
        [
            spread(room[k * TILE + r : k * TILE + r + 1, :]) if used(r, k) else None
            for k in range(TILE)
        ]
        for r in range(TILE)
    ]
    rows = [jnp.where(inside, jnp.where(at[k], 1.0, 0.0), rows[k]) for k in range(TILE)]
    forward = [None] * TILE
    for i, m in enumerate(order):
        later = order[i + 1 :]
        if symmetric:
            kept = jnp.where(at[m], s[m][m], rows[m])
            for k in later:
                kept = jnp.where(at[k], s[m][k], kept)
            forward[m] = kept
        if symmetric and i % 2 == 0:
            n = order[i + 1]
            next_inv = s[m][m] * (1.0 / (s[m][m] * s[n][n] - s[m][n] * s[m][n]))
            inv = 1.0 / s[m][m]
        else:
            inv = next_inv if symmetric else 1.0 / s[m][m]
        lead = {r: s[m][r] if symmetric else s[r][m] for r in later}
        for k in later:
            s[m][k] = s[m][k] * inv
        for r in later:
            for k in later:
                if used(r, k):
                    s[r][k] = s[r][k] - lead[r] * s[m][k]
        rows[m] = rows[m] * inv
        for r in later:
            rows[r] = rows[r] - lead[r] * rows[m]
        yield None
    for i in range(TILE - 1, 0, -1):
        m = order[i]
        for r in order[:i]:
            rows[r] = rows[r] - s[r][m] * rows[m]
    yield rows, forward, inside


def invert_half(a, reverse, room):
    tiles = [a[i * TILE : (i + 1) * TILE, :] for i in range(COUNT)]
    order, places = list(range(TILE)), list(range(COUNT))
    if reverse:
        order, places = order[::-1], places[::-1]
    for n, t in enumerate(places):
        for out in step(tiles, t, order, False, room.at[t % 2]):
            yield None
        rows, _, inside = out
        new = list(tiles)
        for i in places[n + 1 :] + places[: n + 1]:
            new[i] = stack(rows) if i == t else apply_tile(tiles[i], t, rows, inside)
        tiles = new
        yield None
    yield jnp.concatenate(tiles, axis=0)


def eliminate_half(a, reverse, room):
    tiles = [a[i * TILE : (i + 1) * TILE, :] for i in range(COUNT)]
    order, places = list(range(TILE)), list(range(COUNT))
    if reverse:
        order, places = order[::-1], places[::-1]
    for n, t in enumerate(places):
        for out in step(tiles, t, order, True, room.at[2 + t % 2]):
            yield None
        rows, forward, inside = out
        tiles[t] = stack(forward)
        for i in places[n + 1 :]:
            tiles[i] = apply_tile(tiles[i], t, rows, inside)
        yield None
    a = jnp.concatenate(tiles, axis=0)
    rows = lax.broadcasted_iota(jnp.int32, (HB, HB), 0)
    cols = lax.broadcasted_iota(jnp.int32, (HB, HB), 1)
    diag = jnp.sum(jnp.where(rows == cols, a, 0.0), axis=1, keepdims=True)
    scale = 1.0 / jnp.sqrt(diag)
    keep = rows >= cols if reverse else rows <= cols
    factor = jnp.where(keep, a, 0.0) * scale
    yield factor, jnp.where(keep, jnp.where(rows == cols, 1.0, 0.0), a) * scale


def together(*chains):
    results, live = [None] * len(chains), list(range(len(chains)))
    while live:
        for j in list(live):
            value = next(chains[j], live)
            if value is live:
                live.remove(j)
            elif value is not None:
                results[j] = value
    return results


def after(count, action):
    for _ in range(count):
        yield None
    action()
    yield None


class Solve:
    def __init__(self, reverse, room):
        self.reverse, self.room = reverse, room
        self.p, self.q = (1, 0) if reverse else (0, 1)

    def cut(self, x, r, c):
        return x[r * HB : (r + 1) * HB, c * HB : (c + 1) * HB]

    def first(self, gram, *beside):
        p = self.p
        chain = eliminate_half(self.cut(gram, p, p), self.reverse, self.room)
        self.fpp, self.ipp = together(chain, *beside)[0]

    def second(self, gram, top, *beside):
        p, q = self.p, self.q
        self.rpq = dot(self.ipp, self.cut(gram, p, q))
        rest = self.cut(gram, q, q) - dot(self.rpq, self.rpq, 0, 0)
        (self.fqq, self.iqq), self.inv = together(
            eliminate_half(rest, self.reverse, self.room),
            invert_half(self.cut(top, p, p) + self.fpp, self.reverse, self.room),
            *beside,
        )[:2]
        self.fqp = self.cut(top, q, p)
        self.k = dot(self.inv, self.cut(top, p, q) + self.rpq)
        self.rest = self.cut(top, q, q) + self.fqq - dot(self.fqp, self.k)

    def third(self, *beside):
        results = together(invert_half(self.rest, self.reverse, self.room), *beside)
        self.sinv = results[0]
        return results[1:]

    def factor(self):
        zero = jnp.zeros((HB, HB), jnp.float32)
        if self.reverse:
            blocks = [[self.fqq, zero], [self.rpq, self.fpp]]
        else:
            blocks = [[self.fpp, self.rpq], [zero, self.fqq]]
        return jnp.concatenate([jnp.concatenate(b, axis=1) for b in blocks], axis=0)

    def prepare(self, y, t, gap=0):
        half = lambda x, i: x[:, i * HB : (i + 1) * HB]
        wait = [None] * gap
        yp = dot(half(y, self.p), self.ipp, 1, 1)
        yield from wait
        yq = half(y, self.q) - dot(yp, self.rpq)
        yield from wait
        yq = dot(yq, self.iqq, 1, 1)
        yield from wait
        hp = dot(yp + half(t, self.p), self.inv, 1, 1)
        yield from wait
        yield hp, yq + half(t, self.q) - dot(hp, self.fqp, 1, 1)

    def finish(self, hp, hq):
        cq = dot(hq, self.sinv, 1, 1)
        cp = hp - dot(cq, self.k, 1, 1)
        return jnp.concatenate([cq, cp] if self.reverse else [cp, cq], axis=1)


def send(source, target, send_sem, recv_sem, peer):
    copy = pltpu.make_async_remote_copy(
        src_ref=source,
        dst_ref=target,
        send_sem=send_sem,
        recv_sem=recv_sem,
        device_id=peer,
        device_id_type=MESH,
    )
    return copy


def start_all(axis, n, me, source, target, sems):
    copies = []
    for d in range(1, n):
        peer = lax.rem(me + d, n)
        copy = send(source(peer), target, sems[0].at[d - 1], sems[1].at[d - 1], {axis: peer})
        copy.start()
        copies.append(copy)
    return copies


def wait_all(copies):
    for copy in copies:
        copy.wait()


class Pairs:
    def __init__(self, n, me, slot, sems):
        self.n, self.me, self.slot, self.sems = n, me, slot, sems
        self.partner = me + 1 - 2 * lax.rem(me, 2)

    def copy(self, index, block, peer):
        ref = self.slot(block)
        copy = send(ref, ref, self.sems[0].at[index], self.sems[1].at[index], {"col": peer})
        copy.start()
        return copy

    def start(self):
        half = self.n // 2
        self.far = [
            self.copy(d - 1, self.me, lax.rem(self.me + 2 * d, self.n)) for d in range(1, half)
        ]
        self.near = [self.copy(half - 1, self.me, self.partner)]

    def forward(self):
        half = self.n // 2
        for d in range(1, half):
            self.far[d - 1].wait_recv()
            block = lax.rem(self.me + self.n - 2 * d, self.n)
            self.near.append(self.copy(half - 1 + d, block, self.partner))

    def wait(self):
        for copy in self.far:
            copy.wait_send()
        wait_all(self.near)


def kernel(n_row, n_col, a_ref, b_ref, oa_ref, ob_ref, *scratch):
    panel, bw, aw, turned, other, coefs, strips, own_y, got_y, own_c, got_c, both, r_ref, room = scratch[:14]
    pairs_of_sems = [scratch[i : i + 2] for i in range(14, len(scratch), 2)]
    s_scatter, s_row, s_panel, s_bw, s_aw, s_other, s_coefs, s_strips, s_y, s_c, s_both = pairs_of_sems
    rows, cols = a_ref.shape
    window = strips.shape[1]
    start = cols - window
    chunk = rows // n_col
    n_last = NB // window
    row, col = lax.axis_index("row"), lax.axis_index("col")

    barrier = pltpu.get_barrier_semaphore()
    for axis, n, me in (("row", n_row, row), ("col", n_col, col)):
        for d in range(1, n):
            pl.semaphore_signal(
                barrier, inc=1, device_id={axis: lax.rem(me + d, n)}, device_id_type=MESH
            )
    pl.semaphore_wait(barrier, n_row + n_col - 2)

    def part(c):
        return panel.at[row, pl.ds(c * chunk, chunk)]

    def scatter(c):
        source = a_ref.at[pl.ds(c * chunk, chunk), pl.ds(0, NB)]
        return send(source, part(c), s_scatter[0].at[c - 1], s_scatter[1].at[0], {"col": c})

    @pl.when(col == 0)
    def _():
        for c in range(1, n_col):
            scatter(c).start()
        panel[row, pl.ds(0, chunk)] = a_ref[:chunk, :NB]

    bw[row] = b_ref[:, start:].T
    aw[row] = a_ref[:, start:].T
    turned[...] = jnp.concatenate([a_ref[:, :start].T, b_ref[:, :start].T], axis=0).reshape(
        turned.shape
    )
    other[row] = turned[row]

    @pl.when(col != 0)
    def _():
        send(part(col), part(col), s_scatter[0].at[0], s_scatter[1].at[0], {"col": 0}).wait_recv()

    mine = part(col)
    chunks = start_all("row", n_row, row, lambda peer: mine, mine, s_row)
    sent_bw = start_all("row", n_row, row, lambda peer: bw.at[row], bw.at[row], s_bw)
    wait_all(chunks)
    spread_panel = Pairs(n_col, col, lambda c: panel.at[:, pl.ds(c * chunk, chunk)], s_panel)
    spread_panel.start()
    sent_aw = start_all("row", n_row, row, lambda peer: aw.at[row], aw.at[row], s_aw)
    spread_panel.forward()
    spread_panel.wait()

    @pl.when(col == 0)
    def _():
        for c in range(1, n_col):
            scatter(c).wait_send()

    square = jnp.zeros((NB, NB), jnp.float32)
    gram = lax.fori_loop(0, n_row, lambda i, g: g + dot(panel[i], panel[i], 0, 0), square)
    top = panel[0]
    left = Solve(False, room)
    left.first(gram)
    sent_other = start_all("row", n_row, row, lambda peer: turned.at[peer], other.at[row], s_other)
    left.second(gram, top)
    wait_all(sent_bw)

    def beside_third():
        y = dot(bw[0], panel[0])
        for i in range(1, n_row):
            yield from [None] * 8
            y = y + dot(bw[i], panel[i])
        yield from [None] * 8
        yield from left.prepare(y, bw[0], 12)

    coef_b = left.finish(*left.third(beside_third())[0])
    strip = bw[n_row - 1] - dot(coef_b, panel[n_row - 1], 1, 1)
    strips[col] = strip
    spread_strips = Pairs(n_col, col, lambda c: strips.at[c], s_strips)
    spread_strips.start()

    v_rows = panel[row] + jnp.where(row == 0, left.factor(), 0.0)
    wait_all(sent_aw)
    wait_all(sent_other)

    def products(i, y):
        return y + dot(jnp.concatenate([aw[i], other[i]], axis=0), panel[i])

    y = lax.fori_loop(0, n_row, products, jnp.zeros((window + turned.shape[1], NB), jnp.float32))
    (ready,) = together(left.prepare(y, jnp.concatenate([aw[0], other[0]], axis=0)))
    coef = left.finish(*ready)
    coefs[row] = coef[window:]
    sent_coefs = start_all("row", n_row, row, lambda peer: coefs.at[row], coefs.at[row], s_coefs)
    own = jnp.concatenate(
        [
            a_ref[:, start:] - dot(v_rows, coef[:window], 1, 1),
            b_ref[:, start:] - dot(v_rows, coef_b, 1, 1),
        ],
        axis=0,
    )
    own_c[...] = own.reshape(own_c.shape)
    own_y[...] = dot(own, strip).reshape(own_y.shape)
    spread_strips.forward()
    sent_y = start_all("col", n_col, col, lambda peer: own_y.at[peer], got_y.at[col], s_y)
    place = col - (n_col - n_last)
    slot = jnp.maximum(place, 0)

    def last_copies():
        return [
            send(
                own_c.at[lax.rem(col + d, n_col)],
                got_c.at[slot],
                s_c[0].at[d - 1],
                s_c[1].at[slot],
                {"col": lax.rem(col + d, n_col)},
            )
            for d in range(1, n_col)
        ]

    @pl.when(place >= 0)
    def _():
        for copy in last_copies():
            copy.start()
        got_c[slot] = own_c[col]

    spread_strips.wait()

    def add(i, g):
        x = strips[pl.ds(i * n_last, n_last)].reshape(NB, NB)
        return g + dot(x, x, 0, 0)

    gram = lax.fori_loop(0, n_col // n_last, add, square)
    top = strips[n_col - n_last :].reshape(NB, NB)
    right = Solve(True, room)
    spread_both = Pairs(n_col, col, lambda c: both.at[c], s_both)

    def reduce():
        wait_all(sent_y)
        for j in range(n_last):

            @pl.when(place != j)
            def _():
                source = n_col - n_last + j
                copy = send(own_c.at[0], got_c.at[j], s_c[0].at[0], s_c[1].at[j], {"col": source})
                copy.wait_recv()

        total = own_y[col]
        for d in range(1, n_col):
            total = total + got_y[lax.rem(col + d, n_col)]
        both[col] = jnp.concatenate([total] + [got_c[j] for j in range(n_last)], axis=1)
        spread_both.start()

    right.first(gram, after(10 * COUNT // 2, reduce))

    @pl.when(place >= 0)
    def _():
        for copy in last_copies():
            copy.wait_send()

    right.second(gram, top, after(10 * COUNT * 3 // 4, spread_both.forward))
    r_ref[...] = right.factor()
    v_cols = strip + jnp.where(place >= 0, r_ref[pl.ds(slot * window, window), :], 0.0)
    wait_all(sent_coefs)
    spread_both.wait()
    sums = both[...].reshape(2 * rows, 2 * NB)

    def outside():
        all_coefs = coefs[...].reshape(2 * start, NB)
        oa_ref[:, :start] = a_ref[:, :start] - dot(v_rows, all_coefs[:start], 1, 1)
        yield from [None] * 20
        ob_ref[:, :start] = b_ref[:, :start] - dot(v_rows, all_coefs[start:], 1, 1)
        yield None

    ready, _ = right.third(right.prepare(sums[:, :NB], sums[:, NB:], 20), outside())
    done = own_c[...].reshape(2 * rows, window) - dot(right.finish(*ready), v_cols, 1, 1)
    oa_ref[:, start:] = done[:rows]
    ob_ref[:, start:] = done[rows:]


def local(a_matrix, b_matrix):
    rows, cols = a_matrix.shape
    n_row, n_col = lax.axis_size("row"), lax.axis_size("col")
    window = NB * n_row // n_col
    start = cols - window
    share, piece = 2 * rows // n_col, 2 * start // n_row
    f32 = jnp.float32

    def sems(sent, got=None):
        return [pltpu.SemaphoreType.DMA((sent,)), pltpu.SemaphoreType.DMA((got or sent,))]

    scratch = [
        pltpu.VMEM((n_row, rows, NB), f32),
        pltpu.VMEM((n_row, window, NB), f32),
        pltpu.VMEM((n_row, window, NB), f32),
        pltpu.VMEM((n_row, piece, NB), f32),
        pltpu.VMEM((n_row, piece, NB), f32),
        pltpu.VMEM((n_row, piece, NB), f32),
        pltpu.VMEM((n_col, window, NB), f32),
        pltpu.VMEM((n_col, share, NB), f32),
        pltpu.VMEM((n_col, share, NB), f32),
        pltpu.VMEM((n_col, share, window), f32),
        pltpu.VMEM((NB // window, share, window), f32),
        pltpu.VMEM((n_col, share, 2 * NB), f32),
        pltpu.VMEM((NB, NB), f32),
        pltpu.VMEM((4, TILE * TILE, HB), f32),
    ]
    scratch += sems(n_col - 1, 1) + sems(n_row - 1) + sems(n_col - 1)
    scratch += sems(n_row - 1) + sems(n_row - 1) + sems(n_row - 1) + sems(n_row - 1)
    scratch += sems(n_col - 1) + sems(n_col - 1) + sems(n_col - 1, NB // window) + sems(n_col - 1)
    out = jax.ShapeDtypeStruct((rows, cols), f32)
    return pl.pallas_call(
        functools.partial(kernel, n_row, n_col),
        out_shape=[out, out],
        in_specs=[VM, VM],
        out_specs=[VM, VM],
        scratch_shapes=scratch,
        compiler_params=pltpu.CompilerParams(
            collective_id=1, has_side_effects=True, vmem_limit_bytes=LIMIT
        ),
        name="reduction_step",
    )(a_matrix, b_matrix)


def solution(mesh):
    placed = (P("row", "col"), P("row", "col"))
    return jax.shard_map(
        lambda a, b: tuple(local(a, b)),
        mesh=mesh,
        in_specs=placed,
        out_specs=(P("row", "col"), P("row", "col")),
        check_vma=False,
    )
```

profile of v0, /device:TPU:11, one launch (start us, length us, event | category | flops | bytes accessed | tf_op | source)
XLA Modules:
  0.0 81.9 jit_solution(15231661025374116411)
XLA Ops:
  0.6 0.0 copy-start
  0.6 1.0 %copy-done = f32[256,384]{1,0:T(8,128)S(1)} copy-done((f32[256,384]{1,0:T(8,128)S(1)}, f32[256,384]{1,0:T(8,128)}, u32[]{:S(2)}) %copy-start) | copy-done | bytes 393240
  1.6 0.0 copy-start.1
  1.6 1.0 %copy-done.1 = f32[256,384]{1,0:T(8,128)S(1)} copy-done((f32[256,384]{1,0:T(8,128)S(1)}, f32[256,384]{1,0:T(8,128)}, u32[]{:S(2)}) %copy-start.1) | copy-done | bytes 393240
  2.6 77.8 %reduction_step.1 = (f32[256,384]{1,0:T(8,128)S(1)}, f32[256,384]{1,0:T(8,128)S(1)}) custom-call(f32[256,384]{1,0:T(8,128)S(1)} %copy-done, f32[256,384]{1,0:T(8,128)S(1)} %copy-done.1), custom_call_target="tpu_custom_call" | custom-call | tf_op jit(solution)/shard_map/reduction_step/pallas_call | solution.py:482
  80.4 0.7 copy.6
  81.1 0.7 copy.7
Async XLA Ops:
  0.6 1.0 %copy-start = (f32[256,384]{1,0:T(8,128)S(1)}, f32[256,384]{1,0:T(8,128)}, u32[]{:S(2)}) copy-start(f32[256,384]{1,0:T(8,128)} %a_ref.1) | copy-start | bytes 1179652
  1.6 1.0 %copy-start.1 = (f32[256,384]{1,0:T(8,128)S(1)}, f32[256,384]{1,0:T(8,128)}, u32[]{:S(2)}) copy-start(f32[256,384]{1,0:T(8,128)} %b_ref.1) | copy-start | bytes 1179652
where the time goes:
time: 82.1 us; the launch traced here: 81.9 us
  Pallas kernels  77.8 us (95%)
  local copies, waits for them, and re-layouts  3.48 us (4%)
    pallas_call x1, Pallas kernels, local(): pl.pallas_call(functools.partial(kernel, n_row, n_col), out_shape=[out, o...  77.8 us
    unnamed x6, local copies, waits for them, and re-layouts  3.48 us

commit v1 on v0

--- a/solution.py
+++ b/solution.py
@@ -256,22 +256,38 @@
         ]
         self.near = [self.copy(half - 1, self.me, self.partner)]
 
-    def forward(self):
+    def forward(self, use=None):
         half = self.n // 2
         for d in range(1, half):
             self.far[d - 1].wait_recv()
             block = lax.rem(self.me + self.n - 2 * d, self.n)
             self.near.append(self.copy(half - 1 + d, block, self.partner))
-
-    def wait(self):
-        for copy in self.far:
+            if use is not None:
+                use(block)
+
+    def wait(self, use=None):
+        for d, copy in enumerate(self.near):
+            copy.wait_recv()
+            if use is not None:
+                use(lax.rem(self.partner + self.n - 2 * d, self.n))
+        for copy in self.far + self.near:
             copy.wait_send()
-        wait_all(self.near)
-
-
-def kernel(n_row, n_col, a_ref, b_ref, oa_ref, ob_ref, *scratch):
-    panel, bw, aw, turned, other, coefs, strips, own_y, got_y, own_c, got_c, both, r_ref, room = scratch[:14]
-    pairs_of_sems = [scratch[i : i + 2] for i in range(14, len(scratch), 2)]
+
+
+class Gram:
+    def __init__(self, ref):
+        self.ref, self.total = ref, None
+
+    def __call__(self, c):
+        x = self.ref(c)[...].reshape(-1, NB)
+        part = dot(x, x, 0, 0)
+        self.total = part if self.total is None else self.total + part
+
+
+def kernel(n_row, n_col, a_hbm, b_hbm, oa_ref, ob_ref, *scratch):
+    a_ref, b_ref, loaded, own_y, pair_y, sum_y, got_y, s_pair, *scratch = scratch
+    panel, bw, aw, turned, other, coefs, strips, own_c, got_c, both, r_ref, room = scratch[:12]
+    pairs_of_sems = [scratch[i : i + 2] for i in range(12, len(scratch), 2)]
     s_scatter, s_row, s_panel, s_bw, s_aw, s_other, s_coefs, s_strips, s_y, s_c, s_both = pairs_of_sems
     rows, cols = a_ref.shape
     window = strips.shape[1]
@@ -286,27 +302,34 @@
             pl.semaphore_signal(
                 barrier, inc=1, device_id={axis: lax.rem(me + d, n)}, device_id_type=MESH
             )
-    pl.semaphore_wait(barrier, n_row + n_col - 2)
-
-    def part(c):
-        return panel.at[row, pl.ds(c * chunk, chunk)]
-
-    def scatter(c):
-        source = a_ref.at[pl.ds(c * chunk, chunk), pl.ds(0, NB)]
-        return send(source, part(c), s_scatter[0].at[c - 1], s_scatter[1].at[0], {"col": c})
-
-    @pl.when(col == 0)
-    def _():
-        for c in range(1, n_col):
-            scatter(c).start()
-        panel[row, pl.ds(0, chunk)] = a_ref[:chunk, :NB]
-
+    loads = [
+        pltpu.make_async_copy(source, target, loaded.at[i])
+        for i, (source, target) in enumerate([(a_hbm, a_ref), (b_hbm, b_ref)])
+    ]
+    for copy in loads:
+        copy.start()
+    for copy in loads:
+        copy.wait()
     bw[row] = b_ref[:, start:].T
     aw[row] = a_ref[:, start:].T
     turned[...] = jnp.concatenate([a_ref[:, :start].T, b_ref[:, :start].T], axis=0).reshape(
         turned.shape
     )
     other[row] = turned[row]
+    pl.semaphore_wait(barrier, n_row + n_col - 2)
+
+    def part(c):
+        return panel.at[row, pl.ds(c * chunk, chunk)]
+
+    def scatter(c):
+        source = a_ref.at[pl.ds(c * chunk, chunk), pl.ds(0, NB)]
+        return send(source, part(c), s_scatter[0].at[c - 1], s_scatter[1].at[0], {"col": c})
+
+    @pl.when(col == 0)
+    def _():
+        for c in range(1, n_col):
+            scatter(c).start()
+        panel[row, pl.ds(0, chunk)] = a_ref[:chunk, :NB]
 
     @pl.when(col != 0)
     def _():
@@ -316,19 +339,21 @@
     chunks = start_all("row", n_row, row, lambda peer: mine, mine, s_row)
     sent_bw = start_all("row", n_row, row, lambda peer: bw.at[row], bw.at[row], s_bw)
     wait_all(chunks)
-    spread_panel = Pairs(n_col, col, lambda c: panel.at[:, pl.ds(c * chunk, chunk)], s_panel)
+    block = lambda c: panel.at[:, pl.ds(pl.multiple_of(c * chunk, chunk), chunk)]
+    spread_panel = Pairs(n_col, col, block, s_panel)
     spread_panel.start()
     sent_aw = start_all("row", n_row, row, lambda peer: aw.at[row], aw.at[row], s_aw)
-    spread_panel.forward()
-    spread_panel.wait()
+    gram = Gram(block)
+    gram(col)
+    spread_panel.forward(gram)
+    spread_panel.wait(gram)
 
     @pl.when(col == 0)
     def _():
         for c in range(1, n_col):
             scatter(c).wait_send()
 
-    square = jnp.zeros((NB, NB), jnp.float32)
-    gram = lax.fori_loop(0, n_row, lambda i, g: g + dot(panel[i], panel[i], 0, 0), square)
+    gram = gram.total
     top = panel[0]
     left = Solve(False, room)
     left.first(gram)
@@ -351,28 +376,47 @@
     spread_strips.start()
 
     v_rows = panel[row] + jnp.where(row == 0, left.factor(), 0.0)
+
+    def products(ref):
+        zero = jnp.zeros(ref.shape[1:], jnp.float32)
+        return lax.fori_loop(0, n_row, lambda i, y: y + dot(ref[i], panel[i]), zero)
+
+    def coefficients(ref):
+        (ready,) = together(left.prepare(products(ref), ref[0]))
+        return left.finish(*ready)
+
     wait_all(sent_aw)
-    wait_all(sent_other)
-
-    def products(i, y):
-        return y + dot(jnp.concatenate([aw[i], other[i]], axis=0), panel[i])
-
-    y = lax.fori_loop(0, n_row, products, jnp.zeros((window + turned.shape[1], NB), jnp.float32))
-    (ready,) = together(left.prepare(y, jnp.concatenate([aw[0], other[0]], axis=0)))
-    coef = left.finish(*ready)
-    coefs[row] = coef[window:]
-    sent_coefs = start_all("row", n_row, row, lambda peer: coefs.at[row], coefs.at[row], s_coefs)
     own = jnp.concatenate(
         [
-            a_ref[:, start:] - dot(v_rows, coef[:window], 1, 1),
+            a_ref[:, start:] - dot(v_rows, coefficients(aw), 1, 1),
             b_ref[:, start:] - dot(v_rows, coef_b, 1, 1),
         ],
         axis=0,
     )
     own_c[...] = own.reshape(own_c.shape)
     own_y[...] = dot(own, strip).reshape(own_y.shape)
-    spread_strips.forward()
-    sent_y = start_all("col", n_col, col, lambda peer: own_y.at[peer], got_y.at[col], s_y)
+
+    n_chip, chip, core = n_col // 2, col // 2, lax.rem(col, 2)
+    pair = send(
+        own_y.at[:, 1 - core], pair_y, s_pair.at[0], s_pair.at[1], {"col": col + 1 - 2 * core}
+    )
+    pair.start()
+    wait_all(sent_other)
+    coefs[row] = coefficients(other)
+    sent_coefs = start_all("row", n_row, row, lambda peer: coefs.at[row], coefs.at[row], s_coefs)
+    pair.wait()
+    sum_y[...] = own_y[:, core] + pair_y[...]
+    gram = Gram(lambda c: strips.at[c])
+    gram(col)
+    spread_strips.forward(gram)
+    sent_y = []
+    for d in range(1, n_chip):
+        to = lax.rem(chip + d, n_chip)
+        copy = send(
+            sum_y.at[to], got_y.at[chip], s_y[0].at[d - 1], s_y[1].at[d - 1], {"col": 2 * to + core}
+        )
+        copy.start()
+        sent_y.append(copy)
     place = col - (n_col - n_last)
     slot = jnp.maximum(place, 0)
 
@@ -394,13 +438,8 @@
             copy.start()
         got_c[slot] = own_c[col]
 
-    spread_strips.wait()
-
-    def add(i, g):
-        x = strips[pl.ds(i * n_last, n_last)].reshape(NB, NB)
-        return g + dot(x, x, 0, 0)
-
-    gram = lax.fori_loop(0, n_col // n_last, add, square)
+    spread_strips.wait(gram)
+    gram = gram.total
     top = strips[n_col - n_last :].reshape(NB, NB)
     right = Solve(True, room)
     spread_both = Pairs(n_col, col, lambda c: both.at[c], s_both)
@@ -415,9 +454,9 @@
                 copy = send(own_c.at[0], got_c.at[j], s_c[0].at[0], s_c[1].at[j], {"col": source})
                 copy.wait_recv()
 
-        total = own_y[col]
-        for d in range(1, n_col):
-            total = total + got_y[lax.rem(col + d, n_col)]
+        total = sum_y[chip]
+        for d in range(1, n_chip):
+            total = total + got_y[lax.rem(chip + d, n_chip)]
         both[col] = jnp.concatenate([total] + [got_c[j] for j in range(n_last)], axis=1)
         spread_both.start()
 
@@ -460,6 +499,14 @@
         return [pltpu.SemaphoreType.DMA((sent,)), pltpu.SemaphoreType.DMA((got or sent,))]
 
     scratch = [
+        pltpu.VMEM((rows, cols), f32),
+        pltpu.VMEM((rows, cols), f32),
+        pltpu.SemaphoreType.DMA((2,)),
+        pltpu.VMEM((n_col // 2, 2, share, NB), f32),
+        pltpu.VMEM((n_col // 2, share, NB), f32),
+        pltpu.VMEM((n_col // 2, share, NB), f32),
+        pltpu.VMEM((n_col // 2, share, NB), f32),
+        pltpu.SemaphoreType.DMA((2,)),
         pltpu.VMEM((n_row, rows, NB), f32),
         pltpu.VMEM((n_row, window, NB), f32),
         pltpu.VMEM((n_row, window, NB), f32),
@@ -467,8 +514,6 @@
         pltpu.VMEM((n_row, piece, NB), f32),
         pltpu.VMEM((n_row, piece, NB), f32),
         pltpu.VMEM((n_col, window, NB), f32),
-        pltpu.VMEM((n_col, share, NB), f32),
-        pltpu.VMEM((n_col, share, NB), f32),
         pltpu.VMEM((n_col, share, window), f32),
         pltpu.VMEM((NB // window, share, window), f32),
         pltpu.VMEM((n_col, share, 2 * NB), f32),
@@ -477,19 +522,19 @@
     ]
     scratch += sems(n_col - 1, 1) + sems(n_row - 1) + sems(n_col - 1)
     scratch += sems(n_row - 1) + sems(n_row - 1) + sems(n_row - 1) + sems(n_row - 1)
-    scratch += sems(n_col - 1) + sems(n_col - 1) + sems(n_col - 1, NB // window) + sems(n_col - 1)
+    scratch += sems(n_col - 1) + sems(n_col // 2 - 1) + sems(n_col - 1, NB // window) + sems(n_col - 1)
     out = jax.ShapeDtypeStruct((rows, cols), f32)
     return pl.pallas_call(
         functools.partial(kernel, n_row, n_col),
         out_shape=[out, out],
-        in_specs=[VM, VM],
+        in_specs=[pl.BlockSpec(memory_space=pltpu.HBM)] * 2,
         out_specs=[VM, VM],
         scratch_shapes=scratch,
         compiler_params=pltpu.CompilerParams(
             collective_id=1, has_side_effects=True, vmem_limit_bytes=LIMIT
         ),
         name="reduction_step",
-    )(a_matrix, b_matrix)
+    )(*(pltpu.with_memory_space_constraint(x, pltpu.HBM) for x in (a_matrix, b_matrix)))
 
 
 def solution(mesh):

time: 82.1 us -> 77.1 us (0.939)
  Pallas kernels: 77.8 us -> 74.9 us
  local copies, waits for them, and re-layouts: 3.48 us -> 1.49 us
    pallas_call x1, Pallas kernels: 77.8 us -> 74.9 us  [local(): pl.pallas_call(functools.partial(kernel, n_row, n_col), out_shape=[out, o...]
    unnamed x6 -> x2, local copies, waits for them, and re-layouts: 3.48 us -> 1.49 us
where the time goes in v1:
time: 77.1 us; the launch traced here: 77 us
  Pallas kernels  74.9 us (97%)
  local copies, waits for them, and re-layouts  1.49 us (2%)
    pallas_call x1, Pallas kernels, local(): pl.pallas_call(functools.partial(kernel, n_row, n_col), out_shape=[out, o...  74.9 us

profile of v1, /device:TPU:11, one launch (start us, length us, event | category | flops | bytes accessed | tf_op | source)
XLA Modules:
  0.0 77.0 jit_solution(16859149416610335240)
XLA Ops:
  0.6 74.9 %reduction_step.1 = (f32[256,384]{1,0:T(8,128)S(1)}, f32[256,384]{1,0:T(8,128)S(1)}) custom-call(f32[256,384]{1,0:T(8,128)} %a_hbm.1, f32[256,384]{1,0:T(8,128)} %b_hbm.1), custom_call_target="tpu_custom_call" | custom-call | tf_op jit(solution)/shard_map/reduction_step/pallas_call | solution.py:527
  75.5 0.7 copy.6
  76.2 0.7 copy.7

commit v2 on v1

--- a/solution.py
+++ b/solution.py
@@ -338,15 +338,30 @@
     mine = part(col)
     chunks = start_all("row", n_row, row, lambda peer: mine, mine, s_row)
     sent_bw = start_all("row", n_row, row, lambda peer: bw.at[row], bw.at[row], s_bw)
-    wait_all(chunks)
     block = lambda c: panel.at[:, pl.ds(pl.multiple_of(c * chunk, chunk), chunk)]
-    spread_panel = Pairs(n_col, col, block, s_panel)
-    spread_panel.start()
+    spreads = []
+    for d in range(n_row):
+        if d:
+            chunks[d - 1].wait_recv()
+        slot = lambda c, r=lax.rem(row + n_row - d, n_row): panel.at[r, pl.ds(c * chunk, chunk)]
+        spreads.append(Pairs(n_col, col, slot, [s.at[d] for s in s_panel]))
+        spreads[d].start()
     sent_aw = start_all("row", n_row, row, lambda peer: aw.at[row], aw.at[row], s_aw)
     gram = Gram(block)
     gram(col)
-    spread_panel.forward(gram)
-    spread_panel.wait(gram)
+    for each in spreads:
+        each.forward()
+    for d in range(1, n_col // 2):
+        gram(lax.rem(col + n_col - 2 * d, n_col))
+    for d in range(n_col // 2):
+        for each in spreads:
+            each.near[d].wait_recv()
+        gram(lax.rem(each.partner + n_col - 2 * d, n_col))
+    for each in spreads:
+        for copy in each.far + each.near:
+            copy.wait_send()
+    for copy in chunks:
+        copy.wait_send()
 
     @pl.when(col == 0)
     def _():
@@ -457,22 +472,23 @@
         total = sum_y[chip]
         for d in range(1, n_chip):
             total = total + got_y[lax.rem(chip + d, n_chip)]
-        both[col] = jnp.concatenate([total] + [got_c[j] for j in range(n_last)], axis=1)
-        spread_both.start()
-
-    right.first(gram, after(10 * COUNT // 2, reduce))
+        sums.extend([total, jnp.concatenate([got_c[j] for j in range(n_last)], axis=1)])
+
+    sums = []
+    right.first(gram)
 
     @pl.when(place >= 0)
     def _():
         for copy in last_copies():
             copy.wait_send()
 
-    right.second(gram, top, after(10 * COUNT * 3 // 4, spread_both.forward))
+    right.second(gram, top, after(10 * COUNT // 2, reduce))
+    (ready,) = together(right.prepare(*sums))
+    both[col] = jnp.concatenate(ready, axis=1)
+    spread_both.start()
     r_ref[...] = right.factor()
     v_cols = strip + jnp.where(place >= 0, r_ref[pl.ds(slot * window, window), :], 0.0)
     wait_all(sent_coefs)
-    spread_both.wait()
-    sums = both[...].reshape(2 * rows, 2 * NB)
 
     def outside():
         all_coefs = coefs[...].reshape(2 * start, NB)
@@ -481,8 +497,12 @@
         ob_ref[:, :start] = b_ref[:, :start] - dot(v_rows, all_coefs[start:], 1, 1)
         yield None
 
-    ready, _ = right.third(right.prepare(sums[:, :NB], sums[:, NB:], 20), outside())
-    done = own_c[...].reshape(2 * rows, window) - dot(right.finish(*ready), v_cols, 1, 1)
+    right.third(outside())
+    spread_both.forward()
+    spread_both.wait()
+    ready = both[...].reshape(2 * rows, NB)
+    coef = right.finish(ready[:, :HB], ready[:, HB:])
+    done = own_c[...].reshape(2 * rows, window) - dot(coef, v_cols, 1, 1)
     oa_ref[:, start:] = done[:rows]
     ob_ref[:, start:] = done[rows:]
 
@@ -516,11 +536,12 @@
         pltpu.VMEM((n_col, window, NB), f32),
         pltpu.VMEM((n_col, share, window), f32),
         pltpu.VMEM((NB // window, share, window), f32),
-        pltpu.VMEM((n_col, share, 2 * NB), f32),
+        pltpu.VMEM((n_col, share, NB), f32),
         pltpu.VMEM((NB, NB), f32),
         pltpu.VMEM((4, TILE * TILE, HB), f32),
     ]
-    scratch += sems(n_col - 1, 1) + sems(n_row - 1) + sems(n_col - 1)
+    scratch += sems(n_col - 1, 1) + sems(n_row - 1)
+    scratch += [pltpu.SemaphoreType.DMA((n_row, n_col - 1))] * 2
     scratch += sems(n_row - 1) + sems(n_row - 1) + sems(n_row - 1) + sems(n_row - 1)
     scratch += sems(n_col - 1) + sems(n_col // 2 - 1) + sems(n_col - 1, NB // window) + sems(n_col - 1)
     out = jax.ShapeDtypeStruct((rows, cols), f32)

time: 77.1 us -> 75.5 us (0.979)
  Pallas kernels: 74.9 us -> 72.6 us
    pallas_call x1, Pallas kernels: 74.9 us -> 72.6 us  [local(): pl.pallas_call(functools.partial(kernel, n_row, n_col), out_shape=[out, o...]
where the time goes in v2:
time: 75.5 us; the launch traced here: 74.8 us
  Pallas kernels  72.6 us (96%)
  local copies, waits for them, and re-layouts  1.49 us (2%)
    pallas_call x1, Pallas kernels, local(): pl.pallas_call(functools.partial(kernel, n_row, n_col), out_shape=[out, o...  72.6 us

profile of v2, /device:TPU:11, one launch (start us, length us, event | category | flops | bytes accessed | tf_op | source)
XLA Modules:
  0.0 74.8 jit_solution(3831144607244744668)
XLA Ops:
  0.6 72.6 %reduction_step.1 = (f32[256,384]{1,0:T(8,128)S(1)}, f32[256,384]{1,0:T(8,128)S(1)}) custom-call(f32[256,384]{1,0:T(8,128)} %a_hbm.1, f32[256,384]{1,0:T(8,128)} %b_hbm.1), custom_call_target="tpu_custom_call" | custom-call | tf_op jit(solution)/shard_map/reduction_step/pallas_call | solution.py:548
  73.3 0.7 %copy.6 = f32[256,384]{1,0:T(8,128)} copy(f32[256,384]{1,0:T(8,128)S(1)} %get-tuple-element.4) | data formatting | bytes 786432
  74.0 0.7 copy.7
